TPU v7x, 32 devices: a whole 2x2x4 slice. The times are simulated.
32 devices in a mesh: logger: 4 (over y, x), seq: 2 (over core), vocab: 4 (over z).
Axes of the slice: x: 2, y: 2, z: 4, core: 2. Of those that a mesh axis runs over, the one named last changes fastest.
Arguments:
- hidden: bfloat16 [4, 64, 4096], P('logger', ('seq', 'vocab'))
- head_weight: bfloat16 [4, 4096, 4096], P('logger', None, ('seq', 'vocab')), may hold values from -0.09375 to 0.09375
- logged_tokens: int32 [64], replicated, may hold values from 0 to 4095
- logger_share: float32 [4], replicated, may hold values from 0.1 to 1
Outputs:
- log_weight: float32 [4, 64], P('logger', ('seq', 'vocab'))
All inputs are finite; a program needn't handle non-finite values.
Results may differ from a plain program's by a relative error of at most 0.00045.
Values may be sent and summed in bfloat16 or wider, within the bound.
A program may use at most 64 MiB of HBM per device.

v0:
```python
import jax
import jax.numpy as jnp
from jax import lax
from jax.sharding import PartitionSpec as P


def prefix(part, axis, combine, identity):
    place = lax.axis_index(axis)
    gathered = lax.all_gather(part, axis)
    state = jnp.zeros_like(part) + jnp.asarray(identity, part.dtype)

    def one(hop, state):
        return combine(state, lax.dynamic_index_in_dim(gathered, hop, 0, False))

    return lax.fori_loop(0, place, one, state)


def place(buffer, values, start):
    return values


def add_values(earlier, later):
    return earlier + later


def on_device(hidden, head_weight, logged_tokens, logger_share):
    token_rows = hidden[0]
    weight = head_weight[0]
    col_count = weight.shape[1]
    per_device = token_rows.shape[0]
    total_tokens = logged_tokens.shape[0]
    position = lax.axis_index(("seq", "vocab"))
    column_ids = position * col_count + lax.broadcasted_iota(jnp.int32, (1, col_count), 1)
    zeros = jnp.zeros((total_tokens,), jnp.float32)
    start_carry = (zeros, zeros, zeros)
    start = jnp.int32(0)
    logits = jnp.dot(
        lax.all_gather(token_rows, ("seq", "vocab"), axis=0, tiled=True),
        weight,
        preferred_element_type=jnp.float32,
    )
    block_max = jnp.max(logits, axis=1)
    block_sum = jnp.sum(jnp.exp(logits - block_max[:, None]), axis=1)
    block_pick = jnp.sum(jnp.where(logged_tokens[:, None] == column_ids, logits, 0.0), axis=1)
    stats = (
        place(start_carry[0], block_max, start),
        place(start_carry[1], block_sum, start),
        place(start_carry[2], block_pick, start),
    )
    local_max, local_sum, local_pick = stats
    offset = position * per_device
    whole_max = lax.pmax(local_max, ("seq", "vocab"))
    scaled_sum = local_sum * jnp.exp(local_max - whole_max)
    own_sum, own_pick = (
        lax.psum_scatter(scaled_sum, ("seq", "vocab"), scatter_dimension=0, tiled=True),
        lax.psum_scatter(local_pick, ("seq", "vocab"), scatter_dimension=0, tiled=True),
    )
    own_max = lax.dynamic_slice_in_dim(whole_max, offset, per_device)
    logp = own_pick - own_max - jnp.log(own_sum)
    local_cum = jnp.cumsum(logp)
    device_total = jnp.sum(logp)
    earlier_sum = prefix(device_total, ("seq", "vocab"), add_values, jnp.float32(0.0))
    counts = (offset + jnp.arange(per_device) + 1).astype(jnp.float32)
    own_mean = (earlier_sum + local_cum) / counts
    gathered = lax.all_gather(own_mean[None, :], "logger", axis=0, tiled=True)
    prior = jnp.log(logger_share) - jnp.log(jnp.sum(logger_share))
    shifted = prior[:, None] + gathered
    highest = jnp.max(shifted, axis=0)
    mixture = highest + jnp.log(jnp.sum(jnp.exp(shifted - highest[None, :]), axis=0))
    return (own_mean - mixture)[None, :]


def solution(mesh):
    return jax.shard_map(
        on_device,
        mesh=mesh,
        in_specs=(
            P("logger", ("seq", "vocab"), None),
            P("logger", None, ("seq", "vocab")),
            P(),
            P(),
        ),
        out_specs=P("logger", ("seq", "vocab")),
        check_vma=False,
    )
```

profile of v0, /device:TPU:1, one launch (start us, length us, event | category | flops | bytes accessed | tf_op | source)
XLA Modules:
  0.0 94.9 jit_solution(17818057165997192904)
XLA Ops:
  0.0 0.0 copy-start
  0.0 28.0 %all-gather = bf16[1,64,4096]{2,1,0:T(8,128)(2,1)S(1)} all-gather(bf16[1,8,4096]{2,1,0:T(8,128)(2,1)} %param.6), channel_id=2, replica_groups=mesh['logger'=4,'seq'=2,'vocab'=4] {'seq','vocab'}, dimensions={1}, use_global_device_ids=true | all-gather | bytes 589824 | tf_op jit(solution)/shard_map/all_gather | solution.py:38
  28.0 3.1 %fusion.7 = (f32[64]{0:T(128)S(1)}, f32[64,512]{1,0:T(8,128)S(1)}) fusion(bf16[1,4096,512]{2,1,0:T(8,128)(2,1)} %param.7, bf16[1,64,4096]{2,1,0:T(8,128)(2,1)S(1)} %all-gather), kind=kOutput, calls=%fused_computation.17 | convolution fusion | flops 268468160 | bytes 4849920 | tf_op jit(solution)/shard_map/dot_general | solution.py:37
  31.1 0.0 copy-done.1
  31.1 0.2 select_reduce_fusion
  31.3 17.5 %pmax.7 = f32[64]{0:T(128)S(1)} all-reduce(f32[64]{0:T(128)S(1)} %get-tuple-element.45), channel_id=1, replica_groups=mesh['logger'=4,'seq'=2,'vocab'=4] {'seq','vocab'}, use_global_device_ids=true, to_apply=%region_3.4 | all-reduce | flops 64 | bytes 512 | tf_op jit(solution)/shard_map/pmax | solution.py:52
  48.9 13.7 %all-reduce.3 = (f32[64]{0:T(128)S(1)}, f32[64]{0:T(128)S(1)}) all-reduce(f32[64]{0:T(128)S(1)} %exponential_multiply_fusion, f32[64]{0:T(128)S(1)} %get-tuple-element.29), channel_id=4, replica_groups=mesh['logger'=4,'seq'=2,'vocab'=4] {'seq','vocab'}, use_global_device_ids=true, to_apply=%region_5.6.clone | all-reduce | flops 128 | bytes 1024
  62.6 0.0 copy-done
  62.6 0.7 fusion.6
  64.0 0.7 fusion.4
  64.7 0.2 reduce-window.4
  64.9 1.4 %dynamic-update-slice = f32[8]{0:T(128)S(1)} dynamic-update-slice(f32[8]{0:T(128)S(1)} %broadcast.48, f32[1]{0:T(128)} %bitcast.3, u32[]{:T(128)} %bitcast.4) | dynamic-update-slice | bytes 12
  66.3 16.3 %all-reduce = f32[8]{0:T(128)S(1)} all-reduce(f32[8]{0:T(128)S(1)} %dynamic-update-slice), channel_id=1, replica_groups=mesh['logger'=4,'seq'=2,'vocab'=4] {'seq','vocab'}, use_global_device_ids=true, to_apply=%add | all-reduce | flops 8 | bytes 64
  82.6 5.1 %while.10 = (s32[]{:T(128)}, f32[]{:T(128)}, s32[]{:T(128)}, f32[8]{0:T(128)S(1)}, s32[]{:T(128)}, /*index=5*/s32[]{:T(128)}, s32[]{:T(128)}) while((s32[]{:T(128)}, f32[]{:T(128)}, s32[]{:T(128)}, f32[8]{0:T(128)S(1)}, s32[]{:T(128)}, /*index=5*/s32[]{:T(128)}, s32[]{:T(128)}) %tuple.22), condition=%wide.region_8.9_spmd, body=%wide.region_7.8_spmd.sunk | while | flops 6 | bytes 143 | solution.py:15
  82.6 0.6 dynamic_slice.11
  83.9 0.6 dynamic_slice.11
  85.2 0.6 dynamic_slice.11
  86.4 0.6 dynamic_slice.11
  87.7 5.2 %all-gather.1 = f32[4,1,8]{2,1,0:T(1,128)S(1)} all-gather(f32[1,1,8]{2,1,0:T(1,128)S(1)} %fusion.8), channel_id=1, replica_groups=mesh['logger'=4,'seq'=2,'vocab'=4] {'logger'}, dimensions={0}, use_global_device_ids=true | all-gather | bytes 160 | tf_op jit(solution)/shard_map/all_gather | solution.py:65
  92.9 0.0 copy-done.2
  92.9 0.6 reduce_sum.48
  94.2 0.1 add_reduce_fusion
  94.3 0.1 exponential_reduce_fusion.1
  94.4 0.5 bitcast_subtract_fusion
  (7 shorter events, 0.0 us)
Async XLA Ops:
  0.0 62.6 %copy-start = (u32[32]{0:T(128)S(1)}, u32[32]{0:T(128)}, u32[]{:S(2)}) copy-start(u32[32]{0:T(128)} %constant.40) | copy-start | bytes 388
  0.0 31.1 %copy-start.1 = (s32[64]{0:T(128)S(1)}, s32[64]{0:T(128)}, u32[]{:S(2)}) copy-start(s32[64]{0:T(128)} %param.8) | copy-start | bytes 772
  0.0 92.9 %copy-start.2 = (f32[4]{0:T(128)S(1)}, f32[4]{0:T(128)}, u32[]{:S(2)}) copy-start(f32[4]{0:T(128)} %param.9) | copy-start | bytes 52
where the time goes:
time: 95.2 us; the launch traced here: 94.9 us
  blocking collectives  80.7 us (85%)
  local copies, waits for them, and re-layouts  4.51 us (5%)
  matrix products  3.13 us (3%)
  loops' own time  2.63 us (3%)
  other arithmetic  2.46 us (3%)
  between operations  1.46 us (2%)
    unnamed x2, blocking collectives  30 us
    all_gather x1, blocking collectives, on_device(): lax.all_gather(token_rows, ('seq', 'vocab'), axis=0, tiled=True)  28 us
    pmax x1, blocking collectives, on_device(): whole_max = lax.pmax(local_max, ('seq', 'vocab'))  17.5 us
    all_gather x1, blocking collectives, on_device(): gathered = lax.all_gather(own_mean[None, :], 'logger', axis=0, tiled=True)  5.16 us
    dot_general x1, matrix products, on_device(): jnp.dot(lax.all_gather(token_rows, ('seq', 'vocab'), axis=0, tiled=True),...  3.13 us
    another operation x1, loops' own time, prefix(): return lax.fori_loop(0, place, one, state)  2.63 us
    dynamic_slice x4, local copies, waits for them, and re-layouts, one(): return combine(state, lax.dynamic_index_in_dim(gathered, hop, 0, False))  2.45 us
    unnamed x9, local copies, waits for them, and re-layouts  2.06 us

commit v1 on v0

v1 whole, which is shorter than its diff:
```python
import functools

import jax
import jax.numpy as jnp
from jax import lax
from jax.experimental import pallas as pl
from jax.experimental.pallas import tpu as pltpu
from jax.sharding import PartitionSpec as P

MESH = pl.DeviceIdType.MESH
F32 = jnp.float32
CHUNKS = 2


def kernel(n_log, n_seq, n_voc, tok_ref, share_ref, hid_ref, w_ref, out_ref,
           gath, wv, acc, stat, load_sem, w_sem, recv_sem, up_sem, down_sem, side_sem, stat_send, stat_recv):
    my_l, my_s, z = lax.axis_index("logger"), lax.axis_index("seq"), lax.axis_index("vocab")
    group = n_seq * n_voc
    total = n_log * group
    per, depth = gath.shape[1], gath.shape[2]
    cols = wv.shape[1]
    tokens = group * per
    kc = depth // CHUNKS
    place = my_s * n_voc + z
    me = my_l * group + place

    def span(k):
        return pl.ds(k * kc, kc)

    own_load = pltpu.make_async_copy(hid_ref.at[0], gath.at[place], load_sem)
    own_load.start()
    w_loads = [pltpu.make_async_copy(w_ref.at[0, span(k)], wv.at[span(k)], w_sem.at[k]) for k in range(CHUNKS)]
    for copy in w_loads:
        copy.start()

    def coords(j):
        d = lax.rem(me + j, total)
        p = lax.rem(d, group)
        return (d // group, p // n_voc, lax.rem(p, n_voc)), d

    barrier = pltpu.get_barrier_semaphore()
    for j in range(1, total):
        pl.semaphore_signal(barrier, inc=1, device_id=coords(j)[0], device_id_type=MESH)

    row = lax.broadcasted_iota(jnp.int32, (tokens, tokens), 0)
    col = lax.broadcasted_iota(jnp.int32, (tokens, tokens), 1)
    tok = jnp.broadcast_to(tok_ref[...].astype(F32), (tokens, tokens))
    wanted = jnp.sum(jnp.where(row == col, tok, 0.0), axis=1, keepdims=True)
    wanted = wanted.astype(jnp.int32) - place * cols

    own_load.wait()
    pl.semaphore_wait(barrier, total - 1)

    def send(slot, k, sem, target):
        part = gath.at[slot, :, span(k)]
        return pltpu.make_async_remote_copy(
            src_ref=part, dst_ref=part, send_sem=sem.at[slot, k], recv_sem=recv_sem.at[slot, k],
            device_id=target, device_id_type=MESH)

    def up(slot, k):
        return send(slot, k, up_sem, (my_l, my_s, z + 1))

    def down(slot, k):
        return send(slot, k, down_sem, (my_l, my_s, z - 1))

    def side(slot, k, j):
        return send(slot, k, side_sem.at[j - 1], (my_l, lax.rem(my_s + j, n_seq), z))

    def relay(slot, k, go_up, go_down):
        if go_up:
            pl.when(z < n_voc - 1)(lambda: up(slot, k).start())
        if go_down:
            pl.when(z > 0)(lambda: down(slot, k).start())
        for j in range(1, n_seq):
            side(slot, k, j).start()

    for k in range(CHUNKS):
        relay(place, k, True, True)
    for s in range(1, n_voc):
        for k in range(CHUNKS):
            @pl.when(z - s >= 0)
            def _():
                up(place - s, k).wait_recv()
                relay(place - s, k, True, False)

            @pl.when(z + s < n_voc)
            def _():
                down(place + s, k).wait_recv()
                relay(place + s, k, False, True)

    for k in range(CHUNKS):
        for j in range(1, n_seq):
            other = lax.rem(my_s + j, n_seq) * n_voc
            for v in range(n_voc):
                side(other + v, k, j).wait_recv()
        w_loads[k].wait()
        lhs = gath[:, :, k * kc:(k + 1) * kc].astype(F32).reshape(tokens, kc).astype(jnp.bfloat16)
        part = jnp.dot(lhs, wv[k * kc:(k + 1) * kc, :], preferred_element_type=F32)
        if k == 0:
            acc[...] = part
        else:
            acc[...] += part

    logits = acc[...]
    top = jnp.max(logits, axis=1, keepdims=True)
    lse = top + jnp.log(jnp.sum(jnp.exp(logits - top), axis=1, keepdims=True))
    ids = lax.broadcasted_iota(jnp.int32, (tokens, cols), 1)
    pick = jnp.sum(jnp.where(ids == wanted, logits, 0.0), axis=1, keepdims=True)
    lane = lax.broadcasted_iota(jnp.int32, (tokens, 2 * tokens), 1)
    rows = lax.broadcasted_iota(jnp.int32, (tokens, 2 * tokens), 0)
    both = jnp.where(lane == rows, lse, 0.0) + jnp.where(lane == rows + tokens, pick, 0.0)
    stat[me] = jnp.sum(both, axis=0, keepdims=True)

    def stat_copy(j):
        target, _ = coords(j)
        return pltpu.make_async_remote_copy(
            src_ref=stat.at[me], dst_ref=stat.at[me], send_sem=stat_send.at[j], recv_sem=stat_recv.at[me],
            device_id=target, device_id_type=MESH)

    for j in range(1, total):
        stat_copy(j).start()

    for k in range(CHUNKS):
        pl.when(z < n_voc - 1)(lambda: up(place, k).wait_send())
        pl.when(z > 0)(lambda: down(place, k).wait_send())
        for j in range(1, n_seq):
            side(place, k, j).wait_send()
        for s in range(1, n_voc):
            @pl.when(z - s >= 0)
            def _():
                pl.when(z < n_voc - 1)(lambda: up(place - s, k).wait_send())
                for j in range(1, n_seq):
                    side(place - s, k, j).wait_send()

            @pl.when(z + s < n_voc)
            def _():
                pl.when(z > 0)(lambda: down(place + s, k).wait_send())
                for j in range(1, n_seq):
                    side(place + s, k, j).wait_send()

    prior = []
    whole = share_ref[0]
    for l in range(1, n_log):
        whole = whole + share_ref[l]
    for l in range(n_log):
        prior.append(jnp.log(jnp.full((per, 1), share_ref[l], F32)) - jnp.log(jnp.full((per, 1), whole, F32)))

    for j in range(1, total):
        _, d = coords(j)
        pltpu.make_async_remote_copy(
            src_ref=stat.at[d], dst_ref=stat.at[d], send_sem=stat_send.at[j], recv_sem=stat_recv.at[d],
            device_id=coords(j)[0], device_id_type=MESH).wait_recv()

    parts = stat[...].reshape(n_log, group, 2 * tokens)
    high = jnp.max(parts, axis=1, keepdims=True)
    lses = high + jnp.log(jnp.sum(jnp.exp(parts - high), axis=1, keepdims=True))
    picks = jnp.sum(parts, axis=1, keepdims=True)
    wide = lax.broadcasted_iota(jnp.int32, (n_log, 1, 2 * tokens), 2)
    signed = jnp.where(wide < tokens, -lses, picks)
    at = lax.broadcasted_iota(jnp.int32, (per, 2 * tokens), 1)
    at = jnp.where(at < tokens, at, at - tokens)
    limit = place * per + lax.broadcasted_iota(jnp.int32, (per, 2 * tokens), 0)
    keep = at <= limit
    counts = (place * per + 1 + lax.broadcasted_iota(jnp.int32, (per, 1), 0)).astype(F32)
    running = [jnp.sum(jnp.where(keep, signed[l], 0.0), axis=1, keepdims=True) / counts for l in range(n_log)]
    shifted = [prior[l] + running[l] for l in range(n_log)]
    highest = functools.reduce(jnp.maximum, shifted)
    mixture = highest + jnp.log(sum(jnp.exp(s - highest) for s in shifted))
    own = running[0]
    for l in range(1, n_log):
        own = jnp.where(my_l == l, running[l], own)
    r8 = lax.broadcasted_iota(jnp.int32, (per, per), 0)
    c8 = lax.broadcasted_iota(jnp.int32, (per, per), 1)
    out_ref[...] = jnp.sum(jnp.where(r8 == c8, own - mixture, 0.0), axis=0, keepdims=True)

    for j in range(1, total):
        stat_copy(j).wait_send()


def fused(sizes, hidden, head_weight, logged_tokens, logger_share):
    n_log, n_seq, n_voc = sizes
    group = n_seq * n_voc
    total = n_log * group
    per, depth = hidden.shape[1:]
    cols = head_weight.shape[2]
    tokens = logged_tokens.shape[0]
    vmem = pl.BlockSpec(memory_space=pltpu.VMEM)
    return pl.pallas_call(
        functools.partial(kernel, n_log, n_seq, n_voc),
        out_shape=jax.ShapeDtypeStruct((1, per), F32),
        in_specs=[vmem, pl.BlockSpec(memory_space=pltpu.SMEM),
                  pl.BlockSpec(memory_space=pltpu.HBM), pl.BlockSpec(memory_space=pltpu.HBM)],
        out_specs=vmem,
        scratch_shapes=[
            pltpu.VMEM((group, per, depth), jnp.bfloat16),
            pltpu.VMEM((depth, cols), jnp.bfloat16),
            pltpu.VMEM((tokens, cols), F32),
            pltpu.VMEM((total, 1, 2 * tokens), F32),
            pltpu.SemaphoreType.DMA,
            pltpu.SemaphoreType.DMA((CHUNKS,)),
            pltpu.SemaphoreType.DMA((group, CHUNKS)),
            pltpu.SemaphoreType.DMA((group, CHUNKS)),
            pltpu.SemaphoreType.DMA((group, CHUNKS)),
            pltpu.SemaphoreType.DMA((max(n_seq - 1, 1), group, CHUNKS)),
            pltpu.SemaphoreType.DMA((total,)),
            pltpu.SemaphoreType.DMA((total,)),
        ],
        compiler_params=pltpu.CompilerParams(
            collective_id=0, has_side_effects=True, vmem_limit_bytes=32 * 2**20),
    )(logged_tokens.reshape(1, tokens), logger_share, hidden, head_weight)


def general(hidden, head_weight, logged_tokens, logger_share):
    axes = ("seq", "vocab")
    weight = head_weight[0]
    cols, per = weight.shape[1], hidden.shape[1]
    tokens = logged_tokens.shape[0]
    place = lax.axis_index(axes)
    logits = jnp.dot(lax.all_gather(hidden[0], axes, axis=0, tiled=True), weight, preferred_element_type=F32)
    top = jnp.max(logits, axis=1)
    total = jnp.sum(jnp.exp(logits - top[:, None]), axis=1)
    ids = place * cols + lax.broadcasted_iota(jnp.int32, (1, cols), 1)
    pick = jnp.sum(jnp.where(logged_tokens[:, None] == ids, logits, 0.0), axis=1)
    whole = lax.pmax(top, axes)
    total, pick = lax.psum((total * jnp.exp(top - whole), pick), axes)
    logp = pick - whole - jnp.log(total)
    mine = place * per + lax.broadcasted_iota(jnp.int32, (per, 1), 0)
    before = lax.broadcasted_iota(jnp.int32, (1, tokens), 1) <= mine
    running = jnp.sum(jnp.where(before, logp[None, :], 0.0), axis=1) / (mine[:, 0] + 1).astype(F32)
    every = lax.all_gather(running[None, :], "logger", axis=0, tiled=True)
    prior = jnp.log(logger_share) - jnp.log(jnp.sum(logger_share))
    shifted = prior[:, None] + every
    high = jnp.max(shifted, axis=0)
    mixture = high + jnp.log(jnp.sum(jnp.exp(shifted - high[None, :]), axis=0))
    return (running - mixture)[None, :]


def solution(mesh):
    sizes = tuple(mesh.shape[a] for a in ("logger", "seq", "vocab"))

    def on_device(hidden, head_weight, logged_tokens, logger_share):
        small = sizes[1] * sizes[2] == 8 and 2 * logged_tokens.shape[0] == 128
        body = functools.partial(fused, sizes) if small else general
        return body(hidden, head_weight, logged_tokens, logger_share)

    return jax.shard_map(
        on_device,
        mesh=mesh,
        in_specs=(
            P("logger", ("seq", "vocab"), None),
            P("logger", None, ("seq", "vocab")),
            P(),
            P(),
        ),
        out_specs=P("logger", ("seq", "vocab")),
        check_vma=False,
    )
```

time: 95.2 us -> 28.8 us (0.30)
  the two profiles are of different devices: /device:TPU:1 before, /device:TPU:0 now
where the time goes in v1:
time: 28.8 us; the launch traced here: 28.6 us
  Pallas kernels  23.7 us (82%)
  local copies, waits for them, and re-layouts  4.85 us (17%)
    pallas_call x1, Pallas kernels, fused(): pl.pallas_call(functools.partial(kernel, n_log, n_seq, n_voc), out_shape=...  23.7 us
    unnamed x9, local copies, waits for them, and re-layouts  4.85 us

profile of v1, /device:TPU:0, one launch (start us, length us, event | category | flops | bytes accessed | tf_op | source)
XLA Modules:
  0.0 28.6 jit_solution(3041081304076542777)
XLA Ops:
  0.0 0.0 copy-start
  0.0 2.2 %copy-done = bf16[1,4096,512]{2,1,0:T(8,128)(2,1)S(1)} copy-done((bf16[1,4096,512]{2,1,0:T(8,128)(2,1)S(1)}, bf16[1,4096,512]{2,1,0:T(8,128)(2,1)}, u32[]{:S(2)}) %copy-start) | copy-done | bytes 4194328
  2.2 0.0 copy-start.1
  2.2 0.8 %copy-done.1 = bf16[1,8,4096]{2,1,0:T(8,128)(2,1)S(1)} copy-done((bf16[1,8,4096]{2,1,0:T(8,128)(2,1)S(1)}, bf16[1,8,4096]{2,1,0:T(8,128)(2,1)}, u32[]{:S(2)}) %copy-start.1) | copy-done | bytes 65560
  3.0 0.0 copy-start.2
  3.0 0.7 %copy-done.2 = s32[64]{0:T(128)S(1)} copy-done((s32[64]{0:T(128)S(1)}, s32[64]{0:T(128)}, u32[]{:S(2)}) %copy-start.2) | copy-done | bytes 280
  3.7 0.0 copy-start.3
  3.7 0.7 %copy-done.3 = f32[4]{0:T(128)S(1)} copy-done((f32[4]{0:T(128)S(1)}, f32[4]{0:T(128)}, u32[]{:S(2)}) %copy-start.3) | copy-done | bytes 40
  4.3 23.7 %shard_map.46 = f32[1,8]{1,0:T(1,128)S(1)} custom-call(s32[1,64]{1,0:T(1,128)S(1)} %bitcast.1, f32[4]{0:T(128)S(1)} %copy-done.3, bf16[1,8,4096]{2,1,0:T(8,128)(2,1)S(1)} %copy-done.1, bf16[1,4096,512]{2,1,0:T(8,128)(2,1)S(1)} %copy-done), custom_call_target="tpu_custom_call" | custom-call | tf_op jit(solution)/shard_map/pallas_call | solution.py:188
  28.0 0.5 %copy.6 = f32[1,8]{1,0:T(1,128)} copy(f32[1,8]{1,0:T(1,128)S(1)} %shard_map.46) | data formatting | bytes 64
Async XLA Ops:
  0.0 2.2 %copy-start = (bf16[1,4096,512]{2,1,0:T(8,128)(2,1)S(1)}, bf16[1,4096,512]{2,1,0:T(8,128)(2,1)}, u32[]{:S(2)}) copy-start(bf16[1,4096,512]{2,1,0:T(8,128)(2,1)} %w_ref.1) | copy-start | bytes 12582916
  2.2 0.8 %copy-start.1 = (bf16[1,8,4096]{2,1,0:T(8,128)(2,1)S(1)}, bf16[1,8,4096]{2,1,0:T(8,128)(2,1)}, u32[]{:S(2)}) copy-start(bf16[1,8,4096]{2,1,0:T(8,128)(2,1)} %hid_ref.1) | copy-start | bytes 196612
  3.0 0.7 %copy-start.2 = (s32[64]{0:T(128)S(1)}, s32[64]{0:T(128)}, u32[]{:S(2)}) copy-start(s32[64]{0:T(128)} %param.6) | copy-start | bytes 772
  3.7 0.7 %copy-start.3 = (f32[4]{0:T(128)S(1)}, f32[4]{0:T(128)}, u32[]{:S(2)}) copy-start(f32[4]{0:T(128)} %share_ref.1) | copy-start | bytes 52

commit v2 on v1

v2 whole, which is shorter than its diff:
```python
import functools

import jax
import jax.numpy as jnp
from jax import lax
from jax.experimental import pallas as pl
from jax.experimental.pallas import tpu as pltpu
from jax.sharding import PartitionSpec as P

MESH = pl.DeviceIdType.MESH
F32 = jnp.float32
CHUNKS = 2


def kernel(n_log, n_seq, n_voc, tok_ref, share_ref, hid_ref, w_ref, out_ref,
           gath, wv, acc, pair, stat, tok_v, share_v, load_sem, w_sem, recv_sem, far_sem, side_sem,
           pair_send, pair_recv, stat_send, stat_recv):
    my_l, my_s, z = lax.axis_index("logger"), lax.axis_index("seq"), lax.axis_index("vocab")
    group = n_seq * n_voc
    per, depth = gath.shape[1], gath.shape[2]
    cols = wv.shape[1]
    tokens = group * per
    kc = depth // CHUNKS
    place = my_s * n_voc + z
    logs = [my_l] + [lax.rem(my_l + i, n_log) for i in range(1, n_log)]
    seqs = [my_s] + [lax.rem(my_s + a, n_seq) for a in range(1, n_seq)]
    vocs = [z] + [lax.rem(z + b, n_voc) for b in range(1, n_voc)]
    chips = [(i, b) for i in range(n_log) for b in range(n_voc) if i or b]

    barrier = pltpu.get_barrier_semaphore()
    for i, b in chips:
        pl.semaphore_signal(barrier, inc=1, device_id=(logs[i], my_s, vocs[b]), device_id_type=MESH)
    for a in range(1, n_seq):
        pl.semaphore_signal(barrier, inc=1, device_id=(my_l, seqs[a], z), device_id_type=MESH)

    def span(k):
        return pl.ds(k * kc, kc)

    own_load = pltpu.make_async_copy(hid_ref.at[0], gath.at[place], load_sem.at[0])
    tok_load = pltpu.make_async_copy(tok_ref, tok_v, load_sem.at[1])
    share_load = pltpu.make_async_copy(share_ref, share_v, load_sem.at[2])
    w_loads = [pltpu.make_async_copy(w_ref.at[0, span(k)], wv.at[span(k)], w_sem.at[k]) for k in range(CHUNKS)]
    own_load.start()
    tok_load.start()
    share_load.start()
    for copy in w_loads:
        copy.start()
    own_load.wait()
    pl.semaphore_wait(barrier, len(chips) + n_seq - 1)

    def send(src, slot, k, sem, target):
        return pltpu.make_async_remote_copy(
            src_ref=src, dst_ref=gath.at[slot, :, span(k)], send_sem=sem, recv_sem=recv_sem.at[slot, k],
            device_id=target, device_id_type=MESH)

    def rows_of(slot, k):
        return gath.at[slot, :, span(k)]

    def far(b, k):
        return send(rows_of(place, k), place, k, far_sem.at[b - 1, k], (my_l, my_s, vocs[b]))

    def side(a, b, k):
        slot = my_s * n_voc + vocs[b]
        return send(rows_of(slot, k), slot, k, side_sem.at[a - 1, b, k], (my_l, seqs[a], z))

    def arrived(a, b, k):
        slot = seqs[a] * n_voc + vocs[b]
        send(rows_of(slot, k), slot, k, far_sem.at[0, k], (my_l, my_s, z)).wait_recv()

    for k in range(CHUNKS):
        for b in range(1, n_voc):
            far(b, k).start()
        for a in range(1, n_seq):
            side(a, 0, k).start()

    tok_load.wait()
    share_load.wait()
    row = lax.broadcasted_iota(jnp.int32, (tokens, tokens), 0)
    col = lax.broadcasted_iota(jnp.int32, (tokens, tokens), 1)
    tok = jnp.broadcast_to(tok_v[...].astype(F32), (tokens, tokens))
    wanted = jnp.sum(jnp.where(row == col, tok, 0.0), axis=1, keepdims=True)
    wanted = wanted.astype(jnp.int32) - place * cols
    whole = share_v[0]
    for l in range(1, n_log):
        whole = whole + share_v[l]
    prior = [jnp.log(jnp.full((per, 2 * tokens), share_v[l], F32)) - jnp.log(jnp.full((per, 2 * tokens), whole, F32))
             for l in range(n_log)]

    for k in range(CHUNKS):
        for b in range(1, n_voc):
            arrived(0, b, k)
            for a in range(1, n_seq):
                side(a, b, k).start()

    for k in range(CHUNKS):
        for a in range(1, n_seq):
            for b in range(n_voc):
                arrived(a, b, k)
        w_loads[k].wait()
        lhs = gath[:, :, k * kc:(k + 1) * kc].astype(F32).reshape(tokens, kc).astype(jnp.bfloat16)
        part = jnp.dot(lhs, wv[k * kc:(k + 1) * kc, :], preferred_element_type=F32)
        if k == 0:
            acc[...] = part
        else:
            acc[...] += part

    logits = acc[...]
    top = jnp.max(logits, axis=1, keepdims=True)
    lse = top + jnp.log(jnp.sum(jnp.exp(logits - top), axis=1, keepdims=True))
    ids = lax.broadcasted_iota(jnp.int32, (tokens, cols), 1)
    pick = jnp.sum(jnp.where(ids == wanted, logits, 0.0), axis=1, keepdims=True)
    lane = lax.broadcasted_iota(jnp.int32, (tokens, 2 * tokens), 1)
    rows = lax.broadcasted_iota(jnp.int32, (tokens, 2 * tokens), 0)
    both = jnp.where(lane == rows, lse, 0.0) + jnp.where(lane == rows + tokens, pick, 0.0)
    pair[my_s] = jnp.sum(both, axis=0, keepdims=True)

    def pair_copy(a, slot):
        return pltpu.make_async_remote_copy(
            src_ref=pair.at[slot], dst_ref=pair.at[slot], send_sem=pair_send.at[a], recv_sem=pair_recv.at[slot],
            device_id=(my_l, seqs[a], z), device_id_type=MESH)

    for a in range(1, n_seq):
        pair_copy(a, my_s).start()
    for a in range(1, n_seq):
        pair_copy(a, seqs[a]).wait_recv()

    def merged(parts, axis):
        high = jnp.max(parts, axis=axis, keepdims=True)
        lses = high + jnp.log(jnp.sum(jnp.exp(parts - high), axis=axis, keepdims=True))
        return lses, jnp.sum(parts, axis=axis, keepdims=True)

    wide = lax.broadcasted_iota(jnp.int32, (1, 1, 2 * tokens), 2)
    lses, picks = merged(pair[...], 0)
    me = my_l * n_voc + z
    stat[me] = jnp.where(wide < tokens, lses, picks)[0]

    def stat_copy(n, slot):
        return pltpu.make_async_remote_copy(
            src_ref=stat.at[slot], dst_ref=stat.at[slot], send_sem=stat_send.at[n], recv_sem=stat_recv.at[slot],
            device_id=(logs[chips[n][0]], my_s, vocs[chips[n][1]]), device_id_type=MESH)

    for n in range(len(chips)):
        stat_copy(n, me).start()

    for k in range(CHUNKS):
        for b in range(1, n_voc):
            far(b, k).wait_send()
        for a in range(1, n_seq):
            for b in range(n_voc):
                side(a, b, k).wait_send()
    for a in range(1, n_seq):
        pair_copy(a, my_s).wait_send()
    at = lax.broadcasted_iota(jnp.int32, (per, 2 * tokens), 1)
    at = jnp.where(at < tokens, at, at - tokens)
    index = place * per + lax.broadcasted_iota(jnp.int32, (per, 2 * tokens), 0)
    keep = at <= index
    counts = (index + 1).astype(F32)
    for n, (i, b) in enumerate(chips):
        stat_copy(n, logs[i] * n_voc + vocs[b]).wait_recv()

    lses, picks = merged(stat[...].reshape(n_log, n_voc, 2 * tokens), 1)
    signed = jnp.where(wide < tokens, -lses, picks)
    running = [jnp.sum(jnp.where(keep, signed[l], 0.0), axis=1, keepdims=True) / counts for l in range(n_log)]
    shifted = [prior[l] + running[l] for l in range(n_log)]
    highest = functools.reduce(jnp.maximum, shifted)
    mixture = highest + jnp.log(sum(jnp.exp(s - highest) for s in shifted))
    mine = running[0]
    for l in range(1, n_log):
        mine = jnp.where(my_l == l, running[l], mine)
    r8 = lax.broadcasted_iota(jnp.int32, (per, 2 * tokens), 0)
    c8 = lax.broadcasted_iota(jnp.int32, (per, 2 * tokens), 1)
    result = jnp.sum(jnp.where(r8 == c8, mine - mixture, 0.0), axis=0, keepdims=True)
    out_ref[...] = result[:, :per]

    for n in range(len(chips)):
        stat_copy(n, me).wait_send()


def fused(sizes, hidden, head_weight, logged_tokens, logger_share):
    n_log, n_seq, n_voc = sizes
    group = n_seq * n_voc
    per, depth = hidden.shape[1:]
    cols = head_weight.shape[2]
    tokens = logged_tokens.shape[0]
    vmem = pl.BlockSpec(memory_space=pltpu.VMEM)
    return pl.pallas_call(
        functools.partial(kernel, n_log, n_seq, n_voc),
        out_shape=pltpu.VMEM((1, per), F32),
        in_specs=[pl.BlockSpec(memory_space=pltpu.HBM)] * 4,
        out_specs=vmem,
        scratch_shapes=[
            pltpu.VMEM((group, per, depth), jnp.bfloat16),
            pltpu.VMEM((depth, cols), jnp.bfloat16),
            pltpu.VMEM((tokens, cols), F32),
            pltpu.VMEM((n_seq, 1, 2 * tokens), F32),
            pltpu.VMEM((n_log * n_voc, 1, 2 * tokens), F32),
            pltpu.VMEM((1, tokens), jnp.int32),
            pltpu.SMEM((n_log,), F32),
            pltpu.SemaphoreType.DMA((3,)),
            pltpu.SemaphoreType.DMA((CHUNKS,)),
            pltpu.SemaphoreType.DMA((group, CHUNKS)),
            pltpu.SemaphoreType.DMA((n_voc - 1, CHUNKS)),
            pltpu.SemaphoreType.DMA((n_seq - 1, n_voc, CHUNKS)),
            pltpu.SemaphoreType.DMA((n_seq,)),
            pltpu.SemaphoreType.DMA((n_seq,)),
            pltpu.SemaphoreType.DMA((n_log * n_voc,)),
            pltpu.SemaphoreType.DMA((n_log * n_voc,)),
        ],
        compiler_params=pltpu.CompilerParams(
            collective_id=0, has_side_effects=True, vmem_limit_bytes=63 * 2**20),
    )(logged_tokens.reshape(1, tokens), logger_share, hidden, head_weight)


def general(hidden, head_weight, logged_tokens, logger_share):
    axes = ("seq", "vocab")
    weight = head_weight[0]
    cols, per = weight.shape[1], hidden.shape[1]
    tokens = logged_tokens.shape[0]
    place = lax.axis_index(axes)
    logits = jnp.dot(lax.all_gather(hidden[0], axes, axis=0, tiled=True), weight, preferred_element_type=F32)
    top = jnp.max(logits, axis=1)
    total = jnp.sum(jnp.exp(logits - top[:, None]), axis=1)
    ids = place * cols + lax.broadcasted_iota(jnp.int32, (1, cols), 1)
    pick = jnp.sum(jnp.where(logged_tokens[:, None] == ids, logits, 0.0), axis=1)
    whole = lax.pmax(top, axes)
    total, pick = lax.psum((total * jnp.exp(top - whole), pick), axes)
    logp = pick - whole - jnp.log(total)
    mine = place * per + lax.broadcasted_iota(jnp.int32, (per, 1), 0)
    before = lax.broadcasted_iota(jnp.int32, (1, tokens), 1) <= mine
    running = jnp.sum(jnp.where(before, logp[None, :], 0.0), axis=1) / (mine[:, 0] + 1).astype(F32)
    every = lax.all_gather(running[None, :], "logger", axis=0, tiled=True)
    prior = jnp.log(logger_share) - jnp.log(jnp.sum(logger_share))
    shifted = prior[:, None] + every
    high = jnp.max(shifted, axis=0)
    mixture = high + jnp.log(jnp.sum(jnp.exp(shifted - high[None, :]), axis=0))
    return (running - mixture)[None, :]


def solution(mesh):
    sizes = tuple(mesh.shape[a] for a in ("logger", "seq", "vocab"))

    def on_device(hidden, head_weight, logged_tokens, logger_share):
        small = sizes[1:] == (2, 4) and 2 * logged_tokens.shape[0] == 128
        body = functools.partial(fused, sizes) if small else general
        return body(hidden, head_weight, logged_tokens, logger_share)

    return jax.shard_map(
        on_device,
        mesh=mesh,
        in_specs=(
            P("logger", ("seq", "vocab"), None),
            P("logger", None, ("seq", "vocab")),
            P(),
            P(),
        ),
        out_specs=P("logger", ("seq", "vocab")),
        check_vma=False,
    )
```

time: 28.8 us -> 21.5 us (0.75)
  local copies, waits for them, and re-layouts: 4.85 us -> 0.51 us
  Pallas kernels: 23.7 us -> 20.8 us
    unnamed x9 -> x1, local copies, waits for them, and re-layouts: 4.85 us -> 0.51 us
    pallas_call x1, Pallas kernels: 23.7 us -> 20.8 us  [fused(): pl.pallas_call(functools.partial(kernel, n_log, n_seq, n_voc), out_shape=...]
where the time goes in v2:
time: 21.5 us; the launch traced here: 21.3 us
  Pallas kernels  20.8 us (97%)
  local copies, waits for them, and re-layouts  0.51 us (2%)
    pallas_call x1, Pallas kernels, fused(): pl.pallas_call(functools.partial(kernel, n_log, n_seq, n_voc), out_shape=...  20.8 us
    unnamed x1, local copies, waits for them, and re-layouts  0.51 us

profile of v2, /device:TPU:0, one launch (start us, length us, event | category | flops | bytes accessed | tf_op | source)
XLA Modules:
  0.0 21.3 jit_solution(1572471764670814981)
XLA Ops:
  0.0 20.8 %shard_map.46 = f32[1,8]{1,0:T(1,128)S(1)} custom-call(s32[1,64]{1,0:T(1,128)} %bitcast.1, f32[4]{0:T(128)} %share_ref.1, bf16[1,8,4096]{2,1,0:T(8,128)(2,1)} %hid_ref.1, bf16[1,4096,512]{2,1,0:T(8,128)(2,1)} %w_ref.1), custom_call_target="tpu_custom_call" | custom-call | tf_op jit(solution)/shard_map/pallas_call | solution.py:186
  20.8 0.5 %copy.6 = f32[1,8]{1,0:T(1,128)} copy(f32[1,8]{1,0:T(1,128)S(1)} %shard_map.46) | data formatting | bytes 64

commit v3 on v2

--- a/solution.py
+++ b/solution.py
@@ -10,6 +10,7 @@
 MESH = pl.DeviceIdType.MESH
 F32 = jnp.float32
 CHUNKS = 2
+RELAYED = (0,)
 
 
 def kernel(n_log, n_seq, n_voc, tok_ref, share_ref, hid_ref, w_ref, out_ref,
@@ -24,7 +25,10 @@
     place = my_s * n_voc + z
     logs = [my_l] + [lax.rem(my_l + i, n_log) for i in range(1, n_log)]
     seqs = [my_s] + [lax.rem(my_s + a, n_seq) for a in range(1, n_seq)]
-    vocs = [z] + [lax.rem(z + b, n_voc) for b in range(1, n_voc)]
+    half = z // 2
+    vocs = [z, lax.rem(z + 1 + 2 * half, n_voc), lax.rem(z + 2, n_voc), lax.rem(z + 3 - 2 * half, n_voc)]
+    inner = (z > 0) & (z < n_voc - 1)
+    outer = (z == 0) | (z == n_voc - 1)
     chips = [(i, b) for i in range(n_log) for b in range(n_voc) if i or b]
 
     barrier = pltpu.get_barrier_semaphore()
@@ -59,6 +63,10 @@
     def far(b, k):
         return send(rows_of(place, k), place, k, far_sem.at[b - 1, k], (my_l, my_s, vocs[b]))
 
+    def passed(k):
+        slot = my_s * n_voc + vocs[1]
+        return send(rows_of(slot, k), slot, k, far_sem.at[1, k], (my_l, my_s, vocs[3]))
+
     def side(a, b, k):
         slot = my_s * n_voc + vocs[b]
         return send(rows_of(slot, k), slot, k, side_sem.at[a - 1, b, k], (my_l, seqs[a], z))
@@ -68,8 +76,11 @@
         send(rows_of(slot, k), slot, k, far_sem.at[0, k], (my_l, my_s, z)).wait_recv()
 
     for k in range(CHUNKS):
-        for b in range(1, n_voc):
-            far(b, k).start()
+        for b in (1, 2, 3):
+            if b == 2 and k in RELAYED:
+                pl.when(outer)(lambda: far(2, k).start())
+            else:
+                far(b, k).start()
         for a in range(1, n_seq):
             side(a, 0, k).start()
 
@@ -89,6 +100,8 @@
     for k in range(CHUNKS):
         for b in range(1, n_voc):
             arrived(0, b, k)
+            if b == 1 and k in RELAYED:
+                pl.when(inner)(lambda: passed(k).start())
             for a in range(1, n_seq):
                 side(a, b, k).start()
 
@@ -144,7 +157,11 @@
 
     for k in range(CHUNKS):
         for b in range(1, n_voc):
-            far(b, k).wait_send()
+            if b == 2 and k in RELAYED:
+                pl.when(outer)(lambda: far(2, k).wait_send())
+                pl.when(inner)(lambda: passed(k).wait_send())
+            else:
+                far(b, k).wait_send()
         for a in range(1, n_seq):
             for b in range(n_voc):
                 side(a, b, k).wait_send()

time: 21.5 us -> 21 us (0.977)
  Pallas kernels: 20.8 us -> 20.3 us
    pallas_call x1, Pallas kernels: 20.8 us -> 20.3 us  [fused(): pl.pallas_call(functools.partial(kernel, n_log, n_seq, n_voc), out_shape=...]
where the time goes in v3:
time: 21 us; the launch traced here: 20.9 us
  Pallas kernels  20.3 us (97%)
  local copies, waits for them, and re-layouts  0.51 us (2%)
    pallas_call x1, Pallas kernels, fused(): pl.pallas_call(functools.partial(kernel, n_log, n_seq, n_voc), out_shape=...  20.3 us
    unnamed x1, local copies, waits for them, and re-layouts  0.51 us

profile of v3, /device:TPU:0, one launch (start us, length us, event | category | flops | bytes accessed | tf_op | source)
XLA Modules:
  0.0 20.9 jit_solution(9295746234660054187)
XLA Ops:
  0.0 20.3 %shard_map.46 = f32[1,8]{1,0:T(1,128)S(1)} custom-call(s32[1,64]{1,0:T(1,128)} %bitcast.1, f32[4]{0:T(128)} %share_ref.1, bf16[1,8,4096]{2,1,0:T(8,128)(2,1)} %hid_ref.1, bf16[1,4096,512]{2,1,0:T(8,128)(2,1)} %w_ref.1), custom_call_target="tpu_custom_call" | custom-call | tf_op jit(solution)/shard_map/pallas_call | solution.py:203
  20.3 0.5 %copy.6 = f32[1,8]{1,0:T(1,128)} copy(f32[1,8]{1,0:T(1,128)S(1)} %shard_map.46) | data formatting | bytes 64

commit v4 on v3

--- a/solution.py
+++ b/solution.py
@@ -10,6 +10,7 @@
 MESH = pl.DeviceIdType.MESH
 F32 = jnp.float32
 CHUNKS = 2
+EDGES = (0, 3, 8)
 RELAYED = (0,)
 
 
@@ -21,7 +22,7 @@
     per, depth = gath.shape[1], gath.shape[2]
     cols = wv.shape[1]
     tokens = group * per
-    kc = depth // CHUNKS
+    edges = [depth * part // 8 for part in EDGES]
     place = my_s * n_voc + z
     logs = [my_l] + [lax.rem(my_l + i, n_log) for i in range(1, n_log)]
     seqs = [my_s] + [lax.rem(my_s + a, n_seq) for a in range(1, n_seq)]
@@ -38,7 +39,7 @@
         pl.semaphore_signal(barrier, inc=1, device_id=(my_l, seqs[a], z), device_id_type=MESH)
 
     def span(k):
-        return pl.ds(k * kc, kc)
+        return pl.ds(edges[k], edges[k + 1] - edges[k])
 
     own_load = pltpu.make_async_copy(hid_ref.at[0], gath.at[place], load_sem.at[0])
     tok_load = pltpu.make_async_copy(tok_ref, tok_v, load_sem.at[1])
@@ -110,8 +111,8 @@
             for b in range(n_voc):
                 arrived(a, b, k)
         w_loads[k].wait()
-        lhs = gath[:, :, k * kc:(k + 1) * kc].astype(F32).reshape(tokens, kc).astype(jnp.bfloat16)
-        part = jnp.dot(lhs, wv[k * kc:(k + 1) * kc, :], preferred_element_type=F32)
+        lhs = gath[:, :, edges[k]:edges[k + 1]].astype(F32).reshape(tokens, edges[k + 1] - edges[k]).astype(jnp.bfloat16)
+        part = jnp.dot(lhs, wv[edges[k]:edges[k + 1], :], preferred_element_type=F32)
         if k == 0:
             acc[...] = part
         else:
@@ -152,7 +153,7 @@
             src_ref=stat.at[slot], dst_ref=stat.at[slot], send_sem=stat_send.at[n], recv_sem=stat_recv.at[slot],
             device_id=(logs[chips[n][0]], my_s, vocs[chips[n][1]]), device_id_type=MESH)
 
-    for n in range(len(chips)):
+    for n in reversed(range(len(chips))):
         stat_copy(n, me).start()
 
     for k in range(CHUNKS):

time: 21 us -> 21 us (level)
  no operation moved by 1% of the time
where the time goes in v4:
time: 21 us; the launch traced here: 20.9 us
  Pallas kernels  20.4 us (97%)
  local copies, waits for them, and re-layouts  0.51 us (2%)
    pallas_call x1, Pallas kernels, fused(): pl.pallas_call(functools.partial(kernel, n_log, n_seq, n_voc), out_shape=...  20.4 us
    unnamed x1, local copies, waits for them, and re-layouts  0.51 us

profile of v4, /device:TPU:0, one launch (start us, length us, event | category | flops | bytes accessed | tf_op | source)
XLA Modules:
  0.0 20.9 jit_solution(15886852759092440233)
XLA Ops:
  0.0 20.4 %shard_map.46 = f32[1,8]{1,0:T(1,128)S(1)} custom-call(s32[1,64]{1,0:T(1,128)} %bitcast.1, f32[4]{0:T(128)} %share_ref.1, bf16[1,8,4096]{2,1,0:T(8,128)(2,1)} %hid_ref.1, bf16[1,4096,512]{2,1,0:T(8,128)(2,1)} %w_ref.1), custom_call_target="tpu_custom_call" | custom-call | tf_op jit(solution)/shard_map/pallas_call | solution.py:204
  20.4 0.5 %copy.6 = f32[1,8]{1,0:T(1,128)} copy(f32[1,8]{1,0:T(1,128)S(1)} %shard_map.46) | data formatting | bytes 64
